TPU v7x, 32 devices: a whole 2x2x4 slice. The times are simulated.
32 devices in a mesh: row: 4 (over z), col: 8 (over y, x, core).
Axes of the slice: x: 2, y: 2, z: 4, core: 2. Of those that a mesh axis runs over, the one named last changes fastest.
Arguments:
- a_matrix: float32 [1024, 3072], P('row', 'col'), may hold values from -6 to 6
- b_matrix: float32 [1024, 3072], P('row', 'col'), as said below
Outputs:
- a_result: float32 [1024, 3072], P('row', 'col')
- b_result: float32 [1024, 3072], P('row', 'col')
Inputs may be any that keep to these rules, and one draw needn't show every extreme that they name: b_matrix is zero in its first 256 columns and, at the window's columns t, zero in rows below t; its entry in row t at window column t lies between 4 and 8.
All inputs are finite; a program needn't handle non-finite values.
Results may differ from a plain program's by a relative error of at most 0.00023.
Values sent between devices are 32-bit elements; how exact they have to be, the bound alone decides.
A program may use at most 64 MiB of HBM per device.

v0:
```python
import jax
import jax.numpy as jnp
from jax import lax
from jax.sharding import PartitionSpec as P

NB = 256


def broadcast(block, axis, source):
    block = jnp.where(lax.axis_index(axis) == source, block, jnp.zeros_like(block))
    return lax.psum(block, axis)


def product(left_side, right_side):
    return jnp.dot(
        left_side, right_side, precision=lax.Precision.HIGHEST, preferred_element_type=jnp.float32
    )


def tri_solve(factor, values, on_left, transpose):
    return lax.linalg.triangular_solve(
        factor, values, left_side=on_left, lower=True, transpose_a=transpose
    )


def inverse_of(square):
    normal = product(square.T, square)
    factor = jnp.linalg.cholesky(normal)
    first = tri_solve(factor, square.T, True, False)
    return tri_solve(factor, first, True, True)


def lower_from_reversed(gram):
    factor = jnp.linalg.cholesky(gram[::-1, ::-1])
    return factor.T[::-1, ::-1]


def local(a_matrix, b_matrix):
    panel_width = NB
    block_cols = a_matrix.shape[1]
    row_count = lax.axis_size("row")
    window_rows = panel_width * row_count
    window_dev = window_rows // lax.axis_size("col")
    identity = jnp.eye(panel_width, dtype=jnp.float32)
    row_place = lax.axis_index("row")
    col_place = lax.axis_index("col")
    top_flag = (row_place == 0).astype(jnp.float32)
    panel = broadcast(a_matrix[:, :panel_width], "col", 0)
    gram, top_panel = lax.psum((product(panel.T, panel), panel * top_flag), "row")
    factor = jnp.linalg.cholesky(gram)
    q_rows = tri_solve(factor, panel, False, True)
    q_top = tri_solve(factor, top_panel, False, True)
    w_rows = q_rows + top_flag * identity
    sums_a, sums_b = lax.psum((product(w_rows.T, a_matrix), product(w_rows.T, b_matrix)), "row")
    left_inverse = inverse_of(identity + q_top)
    a_left = a_matrix - product(w_rows, product(left_inverse, sums_a))
    b_left = b_matrix - product(w_rows, product(left_inverse, sums_b))
    strip_block = broadcast(b_left, "row", row_count - 1)
    local_cols = jnp.arange(block_cols)
    start_local = block_cols - window_dev
    inside = local_cols >= start_local
    in_window = inside.astype(jnp.float32)
    position = col_place * window_dev + local_cols - start_local
    last_pos = position - (window_rows - panel_width)
    picked = ((jnp.arange(panel_width)[:, None] == last_pos[None, :]) & inside[None, :]).astype(
        jnp.float32
    )
    strip_masked = strip_block * in_window[None, :]
    z_a, z_b, gram_right, strip_last, a_last, b_last = lax.psum(
        (
            product(a_left, strip_masked.T),
            product(b_left, strip_masked.T),
            product(strip_masked, strip_masked.T),
            product(strip_block, picked.T),
            product(a_left, picked.T),
            product(b_left, picked.T),
        ),
        "col",
    )
    right_factor = lower_from_reversed(gram_right)
    q_last = tri_solve(right_factor, strip_last.T, False, False)
    right_inverse = inverse_of(identity + q_last.T)
    w_cols = tri_solve(right_factor, strip_masked, True, True) + picked
    coeff_a = product(tri_solve(right_factor, z_a, False, False) + a_last, right_inverse)
    coeff_b = product(tri_solve(right_factor, z_b, False, False) + b_last, right_inverse)
    a_result = a_left - product(coeff_a, w_cols)
    b_result = b_left - product(coeff_b, w_cols)
    return (a_result, b_result)


def solution(mesh):
    placed = (P("row", "col"), P("row", "col"))
    return jax.shard_map(
        local,
        mesh=mesh,
        in_specs=placed,
        out_specs=(P("row", "col"), P("row", "col")),
        check_vma=False,
    )
```

profile of v0, /device:TPU:0, one launch (start us, length us, event | category | flops | bytes accessed | tf_op | source)
XLA Modules:
  0.0 532.9 jit_solution(867962301768831684)
XLA Ops:
  9.1 58.8 %all-reduce.10.cloned.1.call-done = f32[256,256]{0,1:T(8,128)} async-done(((f32[256,256]{0,1:T(8,128)}), f32[256,256]{0,1:T(8,128)}) %all-reduce.10.cloned.1.call-update) | async-done | bytes 262160 | tf_op jit(solution)/shard_map/psum | solution.py:11
  67.9 2.1 fusion.99
  71.7 33.9 %all-reduce.12.cloned.1.call-done = f32[256,256]{0,1:T(8,128)} async-done(((f32[256,256]{0,1:T(8,128)}), f32[256,256]{0,1:T(8,128)}) %all-reduce.12.cloned.1.call-update) | async-done | bytes 262160 | tf_op jit(solution)/shard_map/psum | solution.py:49
  106.8 11.7 %cholesky.214 = f32[128,128]{1,0:T(8,128)S(1)} custom-call(f32[128,128]{1,0:T(8,128)S(1)} %cholesky.346), custom_call_target="Cholesky" | custom-call | tf_op jit(solution)/shard_map/jit(cholesky)/cholesky | solution.py:50
  118.6 9.8 %custom-call.32 = f32[1,128,128]{1,2,0:T(8,128)S(1)} custom-call(f32[1,128,128]{2,1,0:T(8,128)S(1)} %get-tuple-element.167), custom_call_target="InvertDiagBlocksLowerTriangular" | custom-call | tf_op jit(solution)/shard_map/jit(cholesky)/cholesky | solution.py:50
  128.9 11.7 %cholesky.231 = f32[128,128]{1,0:T(8,128)S(1)} custom-call(f32[128,128]{1,0:T(8,128)S(1)} %convolution_subtract_fusion.17), custom_call_target="Cholesky" | custom-call | tf_op jit(solution)/shard_map/jit(cholesky)/cholesky | solution.py:50
  142.9 4.3 while.19
  143.7 1.4 bitcast_dynamic-update-slice_fusion.8
  145.8 1.4 bitcast_dynamic-update-slice_fusion.8
  147.2 19.7 %custom-call.33 = f32[2,128,128]{1,2,0:T(8,128)S(1)} custom-call(f32[2,128,128]{2,1,0:T(8,128)S(1)} %get-tuple-element.77), custom_call_target="InvertDiagBlocksLowerTriangular" | custom-call | tf_op jit(solution)/shard_map/triangular_solve/custom-call.0 | solution.py:21
  171.9 38.3 %all-reduce.18.cloned.1.call-done = (f32[256,256]{0,1:T(8,128)}, f32[256,384]{1,0:T(8,128)}) async-done(((f32[256,256]{0,1:T(8,128)}, f32[256,384]{1,0:T(8,128)}), (f32[256,256]{0,1:T(8,128)}, f32[256,384]{1,0:T(8,128)})) %all-reduce.18.cloned.1.call-update) | async-done | bytes 655376 | tf_op jit(solution)/shard_map/psum | solution.py:49
  212.8 11.7 %cholesky.248 = f32[128,128]{1,0:T(8,128)S(1)} custom-call(f32[128,128]{1,0:T(8,128)S(1)} %cholesky.349), custom_call_target="Cholesky" | custom-call | tf_op jit(solution)/shard_map/jit(cholesky)/cholesky | solution.py:28
  224.6 9.8 %custom-call.35 = f32[1,128,128]{1,2,0:T(8,128)S(1)} custom-call(f32[1,128,128]{2,1,0:T(8,128)S(1)} %get-tuple-element.163), custom_call_target="InvertDiagBlocksLowerTriangular" | custom-call | tf_op jit(solution)/shard_map/jit(cholesky)/cholesky | solution.py:28
  234.8 11.7 %cholesky.265 = f32[128,128]{1,0:T(8,128)S(1)} custom-call(f32[128,128]{1,0:T(8,128)S(1)} %convolution_subtract_fusion.16), custom_call_target="Cholesky" | custom-call | tf_op jit(solution)/shard_map/jit(cholesky)/cholesky | solution.py:28
  249.3 4.4 while.20
  253.7 19.7 %custom-call.37 = f32[2,128,128]{1,2,0:T(8,128)S(1)} custom-call(f32[2,128,128]{2,1,0:T(8,128)S(1)} %get-tuple-element.80), custom_call_target="InvertDiagBlocksLowerTriangular" | custom-call | tf_op jit(solution)/shard_map/triangular_solve/custom-call.5 | solution.py:21
  276.1 1.4 broadcast_select_fusion
  278.8 42.4 %all-reduce.16.cloned.1.call-done = (f32[256,384]{1,0:T(8,128)}, f32[256,384]{1,0:T(8,128)}) async-done(((f32[256,384]{1,0:T(8,128)}, f32[256,384]{1,0:T(8,128)}), (f32[256,384]{1,0:T(8,128)}, f32[256,384]{1,0:T(8,128)})) %all-reduce.16.cloned.1.call-update) | async-done | bytes 786448 | tf_op jit(solution)/shard_map/psum | solution.py:54
  329.3 1.7 rev.6
  331.1 59.9 %all-reduce.14.cloned.1.call-done = (f32[256,256]{0,1:T(8,128)}, f32[256,256]{1,0:T(8,128)}, f32[256,256]{0,1:T(8,128)}, f32[256,256]{1,0:T(8,128)}, f32[256,256]{0,1:T(8,128)}, /*index=5*/f32[256,256]{1,0:T(8,128)}) async-done(((f32[256,256]{0,1:T(8,128)}, f32[256,256]{1,0:T(8,128)}, f32[256,256]{0,1:T(8,128)}, f32[256,256]{1,0:T(8,128)}, f32[256,256]{0,1:T(8,128)}, /*index=5*/f32[256,256]{1,0:T(8,128)}), ...) | async-done | bytes 1572880 | tf_op jit(solution)/shard_map/psum | solution.py:69
  392.2 11.7 %cholesky.282 = f32[128,128]{1,0:T(8,128)S(1)} custom-call(f32[128,128]{1,0:T(8,128)S(1)} %cholesky.352), custom_call_target="Cholesky" | custom-call | tf_op jit(solution)/shard_map/jit(cholesky)/cholesky | solution.py:34
  404.0 9.8 %custom-call.38 = f32[1,128,128]{1,2,0:T(8,128)S(1)} custom-call(f32[1,128,128]{2,1,0:T(8,128)S(1)} %get-tuple-element.159), custom_call_target="InvertDiagBlocksLowerTriangular" | custom-call | tf_op jit(solution)/shard_map/jit(cholesky)/cholesky | solution.py:34
  414.3 11.7 %cholesky.299 = f32[128,128]{1,0:T(8,128)S(1)} custom-call(f32[128,128]{1,0:T(8,128)S(1)} %convolution_subtract_fusion.15), custom_call_target="Cholesky" | custom-call | tf_op jit(solution)/shard_map/jit(cholesky)/cholesky | solution.py:34
  429.1 4.2 while.21
  433.4 19.9 %custom-call.39 = f32[2,128,128]{1,2,0:T(8,128)S(1)} custom-call(f32[2,128,128]{2,1,0:T(8,128)S(1)} %get-tuple-element.81), custom_call_target="InvertDiagBlocksLowerTriangular" | custom-call | tf_op jit(solution)/shard_map/triangular_solve/custom-call.6 | solution.py:21
  456.9 11.7 %cholesky.316 = f32[128,128]{1,0:T(8,128)S(1)} custom-call(f32[128,128]{1,0:T(8,128)S(1)} %cholesky.355), custom_call_target="Cholesky" | custom-call | tf_op jit(solution)/shard_map/jit(cholesky)/cholesky | solution.py:28
  468.7 9.8 %custom-call.41 = f32[1,128,128]{1,2,0:T(8,128)S(1)} custom-call(f32[1,128,128]{2,1,0:T(8,128)S(1)} %get-tuple-element.155), custom_call_target="InvertDiagBlocksLowerTriangular" | custom-call | tf_op jit(solution)/shard_map/jit(cholesky)/cholesky | solution.py:28
  478.9 11.9 %cholesky.333 = f32[128,128]{1,0:T(8,128)S(1)} custom-call(f32[128,128]{1,0:T(8,128)S(1)} %convolution_subtract_fusion.14), custom_call_target="Cholesky" | custom-call | tf_op jit(solution)/shard_map/jit(cholesky)/cholesky | solution.py:28
  493.6 4.0 while.22
  497.6 19.7 %custom-call.43 = f32[2,128,128]{1,2,0:T(8,128)S(1)} custom-call(f32[2,128,128]{2,1,0:T(8,128)S(1)} %get-tuple-element.84), custom_call_target="InvertDiagBlocksLowerTriangular" | custom-call | tf_op jit(solution)/shard_map/triangular_solve/custom-call.5 | solution.py:21
  522.5 1.4 convolution_subtract_fusion
  524.5 1.4 convolution_subtract_fusion.1
  (172 shorter events, 55.4 us)
Async XLA Ops:
  7.2 60.7 %all-reduce.10.cloned.1.call-start = ((), (), s32[]{:S(2)}) async-start(), calls=%async_computation | async-start | bytes 524288 | tf_op jit(solution)/shard_map/psum | solution.py:11
  7.2 1.0 slice-start
  9.1 96.6 %all-reduce.12.cloned.1.call-start = ((), (), s32[]{:S(2)}) async-start(), calls=%async_computation.1 | async-start | bytes 524288 | tf_op jit(solution)/shard_map/psum | solution.py:49
  70.0 0.9 copy-start
  70.1 140.2 %all-reduce.18.cloned.1.call-start = ((), (), s32[]{:S(2)}) async-start(), calls=%async_computation.4 | async-start | bytes 1310720 | tf_op jit(solution)/shard_map/psum | solution.py:49
  105.6 1.2 copy-start.4
  167.2 1.0 copy-start.3
  169.6 1.0 copy-start.1
  169.6 151.6 %all-reduce.16.cloned.1.call-start = ((), (), s32[]{:S(2)}) async-start(), calls=%async_computation.3 | async-start | bytes 1572864 | tf_op jit(solution)/shard_map/psum | solution.py:54
  210.2 1.3 copy-start.11
  274.5 1.0 copy-start.6
  277.6 113.5 %all-reduce.14.cloned.1.call-start = ((), (), s32[]{:S(2)}) async-start(), calls=%async_computation.2 | async-start | bytes 3145728 | tf_op jit(solution)/shard_map/psum | solution.py:69
  322.2 1.3 copy-start.7
  327.2 1.0 copy-start.2
  391.0 1.2 copy-start.5
  429.1 24.1 %copy-start.10 = (f32[256,256]{1,0:T(8,128)S(1)}, f32[256,256]{1,0:T(8,128)}, u32[]{:S(2)}) copy-start(f32[256,256]{1,0:T(8,128)} %get-tuple-element.137) | copy-start | bytes 786436
  454.8 1.0 copy-start.9
  519.3 1.0 copy-start.8
  521.0 1.0 copy-start.13
  522.5 1.4 copy-start.12
Sparse Core Ops, SparseCore 0:
  11.6 56.2 all-reduce.9
  70.9 34.6 all-reduce.11
  169.7 40.4 all-reduce.17
  277.7 43.4 all-reduce.15
  331.2 59.7 all-reduce.13
where the time goes:
time: 542 us; the launch traced here: 533 us
  waiting for transfers between devices  233 us (43%)
  other arithmetic  220 us (41%)
  matrix products  31.4 us (6%)
  local copies, waits for them, and re-layouts  26.9 us (5%)
  between operations  20.3 us (4%)
    another operation x9, other arithmetic, tri_solve(): lax.linalg.triangular_solve(factor, values, left_side=on_left, lower=True...  79 us
    psum x2, waiting for transfers between devices, local(): lax.psum((product(panel.T, panel), panel * top_flag), 'row')  72.2 us
    another operation x14, other arithmetic, inverse_of(): factor = jnp.linalg.cholesky(normal)  69.4 us
    psum x1, waiting for transfers between devices, local(): lax.psum((product(a_left, strip_masked.T), product(b_left, strip_masked.T...  59.9 us
    psum x1, waiting for transfers between devices, broadcast(): return lax.psum(block, axis)  58.8 us
    psum x1, waiting for transfers between devices, local(): lax.psum((product(w_rows.T, a_matrix), product(w_rows.T, b_matrix)), 'row')  42.4 us
    another operation x7, other arithmetic, lower_from_reversed(): factor = jnp.linalg.cholesky(gram[::-1, ::-1])  34.6 us
    another operation x6, other arithmetic, local(): factor = jnp.linalg.cholesky(gram)  34 us
  transfers between devices with their start and end apart: 5, of which 5 were waited for; matrix products, arithmetic and copies ran while one was open for 1% of the time, Pallas kernels for 0%

commit v1 on v0

--- a/solution.py
+++ b/solution.py
@@ -8,7 +8,7 @@
 
 def broadcast(block, axis, source):
     block = jnp.where(lax.axis_index(axis) == source, block, jnp.zeros_like(block))
-    return lax.psum(block, axis)
+    return jnp.sum(lax.all_gather(block, axis), 0)
 
 
 def product(left_side, right_side):

time: 542 us -> 521 us (0.961)
  waiting for transfers between devices: 233 us -> 212 us
    all_gather x0 -> x2, waiting for transfers between devices: none -> 65.3 us  [broadcast(): return jnp.sum(lax.all_gather(block, axis), 0)]
    psum x1 -> x0, waiting for transfers between devices: 58.8 us -> none  [broadcast(): return lax.psum(block, axis)]
    psum x2 -> x1, waiting for transfers between devices: 72.2 us -> 34.7 us  [local(): lax.psum((product(panel.T, panel), panel * top_flag), 'row')]
    psum x1, waiting for transfers between devices: 42.4 us -> 52.4 us  [local(): lax.psum((product(w_rows.T, a_matrix), product(w_rows.T, b_matrix)), 'row')]
where the time goes in v1:
time: 521 us; the launch traced here: 512 us
  other arithmetic  223 us (43%)
  waiting for transfers between devices  212 us (41%)
  matrix products  31.2 us (6%)
  local copies, waits for them, and re-layouts  24.5 us (5%)
  between operations  20 us (4%)
    another operation x9, other arithmetic, tri_solve(): lax.linalg.triangular_solve(factor, values, left_side=on_left, lower=True...  79.2 us
    another operation x14, other arithmetic, inverse_of(): factor = jnp.linalg.cholesky(normal)  69.3 us
    all_gather x2, waiting for transfers between devices, broadcast(): return jnp.sum(lax.all_gather(block, axis), 0)  65.3 us
    psum x1, waiting for transfers between devices, local(): lax.psum((product(a_left, strip_masked.T), product(b_left, strip_masked.T...  59.5 us
    psum x1, waiting for transfers between devices, local(): lax.psum((product(w_rows.T, a_matrix), product(w_rows.T, b_matrix)), 'row')  52.4 us
    psum x1, waiting for transfers between devices, local(): lax.psum((product(panel.T, panel), panel * top_flag), 'row')  34.7 us
    another operation x7, other arithmetic, lower_from_reversed(): factor = jnp.linalg.cholesky(gram[::-1, ::-1])  34.6 us
    another operation x6, other arithmetic, local(): factor = jnp.linalg.cholesky(gram)  34 us
  transfers between devices with their start and end apart: 5, of which 5 were waited for; matrix products, arithmetic and copies ran while one was open for 1% of the time, Pallas kernels for 0%

profile of v1, /device:TPU:0, one launch (start us, length us, event | category | flops | bytes accessed | tf_op | source)
XLA Modules:
  0.0 511.6 jit_solution(12211430557152174929)
XLA Ops:
  9.1 32.3 %all-gather.5.cloned.1.call-done = f32[2048,256]{0,1:T(8,128)} async-done(((f32[256,256]{0,1:T(8,128)}), f32[2048,256]{0,1:T(8,128)}) %all-gather.5.cloned.1.call-update) | async-done | bytes 2097168 | tf_op jit(solution)/shard_map/all_gather | solution.py:11
  41.4 2.5 copy.22
  46.3 34.7 %all-reduce.7.cloned.1.call-done = f32[256,256]{0,1:T(8,128)} async-done(((f32[256,256]{0,1:T(8,128)}), f32[256,256]{0,1:T(8,128)}) %all-reduce.7.cloned.1.call-update) | async-done | bytes 262160 | tf_op jit(solution)/shard_map/psum | solution.py:49
  83.1 11.7 %cholesky.214 = f32[128,128]{1,0:T(8,128)S(1)} custom-call(f32[128,128]{1,0:T(8,128)S(1)} %cholesky.346), custom_call_target="Cholesky" | custom-call | tf_op jit(solution)/shard_map/jit(cholesky)/cholesky | solution.py:50
  94.8 9.8 %custom-call.32 = f32[1,128,128]{1,2,0:T(8,128)S(1)} custom-call(f32[1,128,128]{2,1,0:T(8,128)S(1)} %get-tuple-element.166), custom_call_target="InvertDiagBlocksLowerTriangular" | custom-call | tf_op jit(solution)/shard_map/jit(cholesky)/cholesky | solution.py:50
  105.2 11.7 %cholesky.231 = f32[128,128]{1,0:T(8,128)S(1)} custom-call(f32[128,128]{1,0:T(8,128)S(1)} %convolution_subtract_fusion.17), custom_call_target="Cholesky" | custom-call | tf_op jit(solution)/shard_map/jit(cholesky)/cholesky | solution.py:50
  119.1 4.6 while.19
  120.2 1.4 bitcast_dynamic-update-slice_fusion.8
  122.3 1.4 bitcast_dynamic-update-slice_fusion.8
  123.7 19.7 %custom-call.33 = f32[2,128,128]{1,2,0:T(8,128)S(1)} custom-call(f32[2,128,128]{2,1,0:T(8,128)S(1)} %get-tuple-element.77), custom_call_target="InvertDiagBlocksLowerTriangular" | custom-call | tf_op jit(solution)/shard_map/triangular_solve/custom-call.0 | solution.py:21
  147.1 52.4 %all-reduce.11.cloned.1.call-done = (f32[256,384]{1,0:T(8,128)}, f32[256,256]{0,1:T(8,128)}, f32[256,384]{1,0:T(8,128)}) async-done(((f32[256,384]{1,0:T(8,128)}, f32[256,256]{0,1:T(8,128)}, f32[256,384]{1,0:T(8,128)}), (f32[256,384]{1,0:T(8,128)}, f32[256,256]{0,1:T(8,128)}, f32[256,384]{1,0:T(8,128)})) %all-reduce.11.cloned.1.call-update) | async-done | bytes 1048592 | tf_op jit(solution)/shard_map/psum | solution.py:54
  202.8 11.7 %cholesky.248 = f32[128,128]{1,0:T(8,128)S(1)} custom-call(f32[128,128]{1,0:T(8,128)S(1)} %cholesky.349), custom_call_target="Cholesky" | custom-call | tf_op jit(solution)/shard_map/jit(cholesky)/cholesky | solution.py:28
  214.6 9.8 %custom-call.35 = f32[1,128,128]{1,2,0:T(8,128)S(1)} custom-call(f32[1,128,128]{2,1,0:T(8,128)S(1)} %get-tuple-element.162), custom_call_target="InvertDiagBlocksLowerTriangular" | custom-call | tf_op jit(solution)/shard_map/jit(cholesky)/cholesky | solution.py:28
  224.9 11.7 %cholesky.265 = f32[128,128]{1,0:T(8,128)S(1)} custom-call(f32[128,128]{1,0:T(8,128)S(1)} %convolution_subtract_fusion.16), custom_call_target="Cholesky" | custom-call | tf_op jit(solution)/shard_map/jit(cholesky)/cholesky | solution.py:28
  239.3 4.2 while.20
  243.5 19.7 %custom-call.37 = f32[2,128,128]{1,2,0:T(8,128)S(1)} custom-call(f32[2,128,128]{2,1,0:T(8,128)S(1)} %get-tuple-element.80), custom_call_target="InvertDiagBlocksLowerTriangular" | custom-call | tf_op jit(solution)/shard_map/triangular_solve/custom-call.5 | solution.py:21
  270.5 33.1 %all-gather.7.cloned.1.call-done = f32[1024,384]{1,0:T(8,128)} async-done(((f32[256,384]{1,0:T(8,128)}), f32[1024,384]{1,0:T(8,128)}) %all-gather.7.cloned.1.call-update) | async-done | bytes 1572880 | tf_op jit(solution)/shard_map/all_gather | solution.py:11
  303.6 1.5 reduce_sum.19
  309.5 1.7 rev.6
  311.3 59.5 %all-reduce.9.cloned.1.call-done = (f32[256,256]{0,1:T(8,128)}, f32[256,256]{1,0:T(8,128)}, f32[256,256]{0,1:T(8,128)}, f32[256,256]{1,0:T(8,128)}, f32[256,256]{0,1:T(8,128)}, /*index=5*/f32[256,256]{1,0:T(8,128)}) async-done(((f32[256,256]{0,1:T(8,128)}, f32[256,256]{1,0:T(8,128)}, f32[256,256]{0,1:T(8,128)}, f32[256,256]{1,0:T(8,128)}, f32[256,256]{0,1:T(8,128)}, /*index=5*/f32[256,256]{1,0:T(8,128)}), ...) | async-done | bytes 1572880 | tf_op jit(solution)/shard_map/psum | solution.py:69
  372.9 11.7 %cholesky.282 = f32[128,128]{1,0:T(8,128)S(1)} custom-call(f32[128,128]{1,0:T(8,128)S(1)} %cholesky.352), custom_call_target="Cholesky" | custom-call | tf_op jit(solution)/shard_map/jit(cholesky)/cholesky | solution.py:34
  384.7 9.8 %custom-call.38 = f32[1,128,128]{1,2,0:T(8,128)S(1)} custom-call(f32[1,128,128]{2,1,0:T(8,128)S(1)} %get-tuple-element.158), custom_call_target="InvertDiagBlocksLowerTriangular" | custom-call | tf_op jit(solution)/shard_map/jit(cholesky)/cholesky | solution.py:34
  395.0 11.7 %cholesky.299 = f32[128,128]{1,0:T(8,128)S(1)} custom-call(f32[128,128]{1,0:T(8,128)S(1)} %convolution_subtract_fusion.15), custom_call_target="Cholesky" | custom-call | tf_op jit(solution)/shard_map/jit(cholesky)/cholesky | solution.py:34
  409.8 4.2 while.21
  414.1 20.1 %custom-call.39 = f32[2,128,128]{1,2,0:T(8,128)S(1)} custom-call(f32[2,128,128]{2,1,0:T(8,128)S(1)} %get-tuple-element.81), custom_call_target="InvertDiagBlocksLowerTriangular" | custom-call | tf_op jit(solution)/shard_map/triangular_solve/custom-call.6 | solution.py:21
  437.1 11.7 %cholesky.316 = f32[128,128]{1,0:T(8,128)S(1)} custom-call(f32[128,128]{1,0:T(8,128)S(1)} %cholesky.355), custom_call_target="Cholesky" | custom-call | tf_op jit(solution)/shard_map/jit(cholesky)/cholesky | solution.py:28
  448.9 9.8 %custom-call.41 = f32[1,128,128]{1,2,0:T(8,128)S(1)} custom-call(f32[1,128,128]{2,1,0:T(8,128)S(1)} %get-tuple-element.154), custom_call_target="InvertDiagBlocksLowerTriangular" | custom-call | tf_op jit(solution)/shard_map/jit(cholesky)/cholesky | solution.py:28
  459.2 11.9 %cholesky.333 = f32[128,128]{1,0:T(8,128)S(1)} custom-call(f32[128,128]{1,0:T(8,128)S(1)} %convolution_subtract_fusion.14), custom_call_target="Cholesky" | custom-call | tf_op jit(solution)/shard_map/jit(cholesky)/cholesky | solution.py:28
  473.7 4.0 while.22
  477.8 19.7 %custom-call.43 = f32[2,128,128]{1,2,0:T(8,128)S(1)} custom-call(f32[2,128,128]{2,1,0:T(8,128)S(1)} %get-tuple-element.84), custom_call_target="InvertDiagBlocksLowerTriangular" | custom-call | tf_op jit(solution)/shard_map/triangular_solve/custom-call.5 | solution.py:21
  501.5 1.4 convolution_subtract_fusion
  503.5 1.4 convolution_subtract_fusion.1
  (164 shorter events, 55.2 us)
Async XLA Ops:
  7.2 34.2 %all-gather.5.cloned.1.call-start = ((), (), s32[]{:S(2)}) async-start(), calls=%async_computation.1 | async-start | bytes 2359296 | tf_op jit(solution)/shard_map/all_gather | solution.py:11
  9.1 71.9 %all-reduce.7.cloned.1.call-start = ((), (), s32[]{:S(2)}) async-start(), calls=%async_computation | async-start | bytes 524288 | tf_op jit(solution)/shard_map/psum | solution.py:49
  45.5 154.0 %all-reduce.11.cloned.1.call-start = ((), (), s32[]{:S(2)}) async-start(), calls=%async_computation.4 | async-start | bytes 2097152 | tf_op jit(solution)/shard_map/psum | solution.py:54
  83.1 61.2 %copy-start = (f32[256,384]{1,0:T(8,128)S(1)}, f32[256,384]{1,0:T(8,128)}, u32[]{:S(2)}) copy-start(f32[256,384]{1,0:T(8,128)} %param.11) | copy-start | bytes 1179652
  104.9 40.8 %copy-start.1 = (f32[256,384]{1,0:T(8,128)S(1)}, f32[256,384]{1,0:T(8,128)}, u32[]{:S(2)}) copy-start(f32[256,384]{1,0:T(8,128)} %param.12) | copy-start | bytes 1179652
  147.1 156.5 %all-gather.7.cloned.1.call-start = ((), (), s32[]{:S(2)}) async-start(), calls=%async_computation.2 | async-start | bytes 1966080 | tf_op jit(solution)/shard_map/all_gather | solution.py:11
  224.6 40.3 %copy-start.3 = (f32[256,384]{1,0:T(8,128)S(1)}, f32[256,384]{1,0:T(8,128)}, u32[]{:S(2)}) copy-start(f32[256,384]{1,0:T(8,128)} %get-tuple-element.142) | copy-start | bytes 1179652
  264.7 3.5 copy-start.2
  267.0 103.9 %all-reduce.9.cloned.1.call-start = ((), (), s32[]{:S(2)}) async-start(), calls=%async_computation.3 | async-start | bytes 3145728 | tf_op jit(solution)/shard_map/psum | solution.py:69
  394.7 39.4 %copy-start.6 = (f32[256,256]{1,0:T(8,128)S(1)}, f32[256,256]{1,0:T(8,128)}, u32[]{:S(2)}) copy-start(f32[256,256]{1,0:T(8,128)} %get-tuple-element.137) | copy-start | bytes 786436
  409.8 26.2 %copy-start.5 = (f32[256,256]{1,0:T(8,128)S(1)}, f32[256,256]{1,0:T(8,128)}, u32[]{:S(2)}) copy-start(f32[256,256]{1,0:T(8,128)} %get-tuple-element.139) | copy-start | bytes 786436
  473.7 26.1 %copy-start.4 = (f32[256,256]{1,0:T(8,128)S(1)}, f32[256,256]{1,0:T(8,128)}, u32[]{:S(2)}) copy-start(f32[256,256]{1,0:T(8,128)} %get-tuple-element.135) | copy-start | bytes 786436
  497.8 3.1 copy-start.8
  499.5 3.3 copy-start.7
Sparse Core Ops, SparseCore 0:
  10.4 30.8 all-gather.4
  45.6 35.2 all-reduce.6
  147.2 52.2 all-reduce.10
  267.1 36.4 all-gather.6
  311.4 59.3 all-reduce.8
